TPU v7x, 32 devices: a whole 2x2x4 slice. The times are simulated.
32 devices in a mesh: dp: 8 (over z, x), expert: 4 (over y, core).
Axes of the slice: x: 2, y: 2, z: 4, core: 2. Of those that a mesh axis runs over, the one named last changes fastest.
Arguments:
- tokens: bfloat16 [4096, 3584], P('dp'), may hold values from -6 to 6
- grad_out: bfloat16 [4096, 3584], P('dp'), may hold values from -6 to 6
- route_rows: int32 [4096], P('dp'), may hold values from 0 to 511, as said below
- route_gate: float32 [4096], P('dp'), may hold values from 0.1 to 1
- block_count: int32 [8], P('dp'), may hold values from 0 to 4, as said below
- gate_weight: bfloat16 [3584, 2048], P('dp', 'expert'), may hold values from -0.125 to 0.125
- up_weight: bfloat16 [3584, 2048], P('dp', 'expert'), may hold values from -0.125 to 0.125
- down_weight_t: bfloat16 [3584, 2048], P('dp', 'expert'), may hold values from -0.125 to 0.125
Outputs:
- grad_tokens: bfloat16 [4096, 3584], P('dp', 'expert')
- grad_gate_weight: float32 [3584, 2048], P('dp', 'expert')
- grad_up_weight: float32 [3584, 2048], P('dp', 'expert')
Inputs may be any that keep to these rules, and one draw needn't show every extreme that they name: `route_rows`: each index of dp holds 512 entries that are a permutation of 0 to 511. Slots 0 to block_count * 128 - 1 of an index of dp are live, its other slots empty; some index has all 4 blocks live and some index none.
All inputs are finite; a program needn't handle non-finite values.
Results may differ from a plain program's by a relative error of at most 0.017.
Values may be sent and summed in bfloat16 or wider, within the bound.
A program may use at most 64 MiB of HBM per device.

v0:
```python
import jax
import jax.numpy as jnp
from jax import lax
from jax.sharding import PartitionSpec as P

BLOCK = 128


ROWS_CONTRACT = (((0,), (0,)), ((), ()))
COLS_CONTRACT = (((1,), (1,)), ((), ()))


def local(
    tokens, grad_out, route_rows, route_gate, block_count, gate_weight, up_weight, down_weight_t
):
    block_rows = BLOCK
    hidden_width = gate_weight.shape[1]
    slot_count = route_rows.shape[0]
    feature_count = tokens.shape[1]
    live_blocks = block_count[0]
    token_slots = jnp.take(tokens, route_rows, axis=0)
    gate_panel, up_panel, down_panel = (
        lax.all_gather(gate_weight, "dp", axis=0, tiled=True),
        lax.all_gather(up_weight, "dp", axis=0, tiled=True),
        lax.all_gather(down_weight_t, "dp", axis=0, tiled=True),
    )

    def backward_rows(rows_block):
        cotangent_block = jnp.take(grad_out, rows_block, axis=0)
        return jnp.dot(cotangent_block, down_panel, preferred_element_type=jnp.float32)

    both_panels = jnp.concatenate([gate_panel, up_panel], axis=1)

    def slot_grads(block_index):
        offset = block_index * block_rows
        rows_block = lax.dynamic_slice_in_dim(route_rows, offset, block_rows, 0)
        token_block = lax.dynamic_slice_in_dim(token_slots, offset, block_rows, 0)
        weight_block = lax.dynamic_slice_in_dim(route_gate, offset, block_rows, 0)
        projected = jnp.dot(token_block, both_panels, preferred_element_type=jnp.float32)
        gate_val = projected[:, :hidden_width]
        up_val = projected[:, hidden_width:]
        hidden_grad = weight_block[:, None] * backward_rows(rows_block)
        gate_sigmoid = jax.nn.sigmoid(gate_val)
        grad_up = hidden_grad * (gate_val * gate_sigmoid)
        grad_gate = hidden_grad * up_val * gate_sigmoid * (1.0 + gate_val * (1.0 - gate_sigmoid))
        return jnp.concatenate([grad_gate, grad_up], axis=1).astype(jnp.bfloat16)

    def input_block(grads_block):
        return lax.dot_general(
            grads_block, both_panels, COLS_CONTRACT, preferred_element_type=jnp.float32
        )

    empty_grads = jnp.zeros((slot_count, 2 * hidden_width), jnp.bfloat16)
    empty_inputs = jnp.zeros((slot_count, feature_count), jnp.float32)

    def step_both(block_index, running):
        grads_buffer, input_buffer = running
        grads_block = slot_grads(block_index)
        offset = block_index * block_rows
        grads_buffer = lax.dynamic_update_slice_in_dim(grads_buffer, grads_block, offset, 0)
        input_buffer = lax.dynamic_update_slice_in_dim(
            input_buffer, input_block(grads_block), offset, 0
        )
        return (grads_buffer, input_buffer)

    grads_buffer, input_buffer = lax.fori_loop(
        0, live_blocks, step_both, (empty_grads, empty_inputs)
    )
    weight_share = lax.psum_scatter(
        lax.dot_general(
            token_slots, grads_buffer, ROWS_CONTRACT, preferred_element_type=jnp.float32
        ),
        "dp",
        scatter_dimension=0,
        tiled=True,
    )
    summed_inputs = lax.psum_scatter(
        input_buffer.astype(jnp.bfloat16), "expert", scatter_dimension=1, tiled=True
    )
    grad_tokens = jnp.zeros(summed_inputs.shape, jnp.bfloat16).at[route_rows].set(summed_inputs)
    grad_scale = float(lax.axis_size("dp") * slot_count) ** (-0.5)
    grad_gate_weight = weight_share[:, :hidden_width] * grad_scale
    grad_up_weight = weight_share[:, hidden_width:] * grad_scale
    return (grad_tokens, grad_gate_weight, grad_up_weight)


def solution(mesh):
    in_specs = (
        P("dp", None),
        P("dp", None),
        P("dp"),
        P("dp"),
        P("dp"),
        P("dp", "expert"),
        P("dp", "expert"),
        P("dp", "expert"),
    )
    out_specs = (P("dp", "expert"), P("dp", "expert"), P("dp", "expert"))
    return jax.shard_map(local, mesh=mesh, in_specs=in_specs, out_specs=out_specs, check_vma=False)
```

profile of v0, /device:TPU:0, one launch (start us, length us, event | category | flops | bytes accessed | tf_op | source)
XLA Modules:
  0.0 598.5 jit_solution(2715963036306778996)
XLA Ops:
  7.2 0.7 all-gather.6.cloned.1.call-update
  7.9 0.7 all-gather.8.cloned.1.call-update
  8.7 0.7 all-gather.4.cloned.1.call-update
  9.4 0.7 compare_select_fusion.1
  10.1 10.4 %gather_fusion.1 = bf16[512,3584]{1,0:T(8,128)(2,1)} fusion(bf16[512,3584]{1,0:T(8,128)(2,1)} %param.10, s32[1024]{0:T(1024)S(1)} %pad_clamp_fusion.1), kind=kCustom, calls=%fused_computation.1 | custom fusion | bytes 7342080 | tf_op jit(solution)/shard_map/jit(_take)/gather | solution.py:21
  20.6 4.5 broadcast_select_fusion
  25.0 54.7 %all-gather.6.cloned.1.call-done = bf16[3584,512]{1,0:T(8,128)(2,1)} async-done(((bf16[448,512]{1,0:T(8,128)(2,1)}), bf16[3584,512]{1,0:T(8,128)(2,1)}) %all-gather.6.cloned.1.call-update) | async-done | bytes 3670032 | tf_op jit(solution)/shard_map/all_gather | solution.py:23
  79.7 67.5 %all-gather.8.cloned.1.call-done = bf16[3584,512]{1,0:T(8,128)(2,1)} async-done(((bf16[448,512]{1,0:T(8,128)(2,1)}), bf16[3584,512]{1,0:T(8,128)(2,1)}) %all-gather.8.cloned.1.call-update) | async-done | bytes 3670032 | tf_op jit(solution)/shard_map/all_gather | solution.py:24
  147.2 7.1 %pad_maximum_fusion.2 = bf16[3584,1024]{1,0:T(8,128)(2,1)} fusion(bf16[3584,512]{1,0:T(8,128)(2,1)} %all-gather.8.cloned.1.call-done, bf16[3584,512]{1,0:T(8,128)(2,1)} %all-gather.6.cloned.1.call-done), kind=kLoop, calls=%fused_computation.24 | loop fusion | flops 14680064 | bytes 14680064 | tf_op jit(solution)/shard_map/concatenate | solution.py:32
  154.3 60.4 %all-gather.4.cloned.1.call-done = bf16[3584,512]{1,0:T(8,128)(2,1)} async-done(((bf16[448,512]{1,0:T(8,128)(2,1)}), bf16[3584,512]{1,0:T(8,128)(2,1)}) %all-gather.4.cloned.1.call-update) | async-done | bytes 3670032 | tf_op jit(solution)/shard_map/all_gather | solution.py:25
  214.8 2.1 broadcast_in_dim.38
  217.0 43.3 %while.12 = (s32[]{:T(128)}, bf16[512,1024]{1,0:T(8,128)(2,1)S(1)}, bf16[512,3584]{1,0:T(8,128)(2,1)}, s32[]{:T(128)}, f32[512]{0:T(512)}, /*index=5*/s32[512]{0...) while((s32[]{:T(128)}, bf16[512,1024]{1,0:T(8,128)(2,1)S(1)}, ...), condition=%wide.region_1.2_spmd, body=%wide.region_0.1_spmd.sunk | while | flops 2351236864 | bytes 55320572 | solution.py:66
  217.6 0.8 dynamic_slice.16
  218.5 4.5 fusion.31
  223.0 4.5 gather_fusion
  227.5 2.9 fusion.32
  230.7 5.7 convolution_dynamic-update-slice_fusion.2
  236.4 1.9 copy-done.1
  238.9 0.8 dynamic_slice.16
  239.8 4.5 fusion.31
  244.3 4.5 gather_fusion
  248.8 2.9 fusion.32
  252.0 5.7 convolution_dynamic-update-slice_fusion.2
  257.7 1.9 copy-done.1
  260.2 6.0 %copy.11 = bf16[512,3584]{0,1:T(8,128)(2,1)} copy(bf16[512,3584]{1,0:T(8,128)(2,1)} %get-tuple-element.57) | data formatting | bytes 7340032
  266.2 0.2 reduce-scatter.5.cloned.1.call-start
  266.5 9.3 %fusion.14 = f32[3584,1024]{1,0:T(8,128)} fusion(bf16[512,3584]{1,0:T(8,128)(2,1)} %get-tuple-element.202, bf16[512,1024]{1,0:T(8,128)(2,1)S(1)} %get-tuple-element.58), kind=kOutput, calls=%fused_computation.33 | convolution fusion | flops 3758096384 | bytes 19398656 | tf_op jit(solution)/shard_map/dot_general | solution.py:70
  275.8 72.9 %reduce-scatter.7.cloned.1.call-done = bf16[896,512]{1,0:T(8,128)(2,1)} async-done(((bf16[3584,512]{1,0:T(8,128)(2,1)}), bf16[896,512]{1,0:T(8,128)(2,1)}) %reduce-scatter.7.cloned.1.call-update) | async-done | bytes 917520
  348.7 1.5 copy.12
  350.2 3.6 scatter_custom_fusion
  353.9 235.2 %reduce-scatter.5.cloned.1.call-done = f32[448,1024]{1,0:T(8,128)} async-done(((f32[3584,1024]{1,0:T(8,128)}), f32[448,1024]{1,0:T(8,128)}) %reduce-scatter.5.cloned.1.call-update) | async-done | bytes 1835024 | tf_op jit(solution)/shard_map/reduce_scatter | solution.py:69
  589.1 2.9 slice_multiply_fusion.1
  (23 shorter events, 0.9 us)
Async XLA Ops:
  7.2 72.6 %all-gather.6.cloned.1.call-start = ((), (), s32[]{:S(2)}) async-start(), calls=%async_computation.3 | async-start | bytes 4128768 | tf_op jit(solution)/shard_map/all_gather | solution.py:23
  7.9 139.3 %all-gather.8.cloned.1.call-start = ((), (), s32[]{:S(2)}) async-start(), calls=%async_computation.4 | async-start | bytes 4128768 | tf_op jit(solution)/shard_map/all_gather | solution.py:24
  8.6 206.0 %all-gather.4.cloned.1.call-start = ((), (), s32[]{:S(2)}) async-start(), calls=%async_computation.2 | async-start | bytes 4128768 | tf_op jit(solution)/shard_map/all_gather | solution.py:25
  9.4 339.3 %reduce-scatter.7.cloned.1.call-start = ((), (), s32[]{:S(2)}) async-start(), calls=%async_computation.6 | async-start | bytes 4587520
  10.1 10.4 %copy-start.2 = (s32[512]{0:T(512)S(1)}, s32[512]{0:T(512)}, u32[]{:S(2)}) copy-start(s32[512]{0:T(512)} %param.12) | copy-start | bytes 6148
  227.5 3.1 copy-start
  236.4 1.9 copy-start.1
  248.8 3.1 copy-start
  257.7 1.9 copy-start.1
  266.2 322.9 %reduce-scatter.5.cloned.1.call-start = ((), (), s32[]{:S(2)}) async-start(), calls=%async_computation.5 | async-start | bytes 16515072 | tf_op jit(solution)/shard_map/reduce_scatter | solution.py:69
Sparse Core Ops, SparseCore 0:
  10.2 69.4 all-gather.5
  81.9 65.2 all-gather.7
  149.4 65.2 all-gather.3
  266.4 82.2 reduce-scatter.6
  352.5 236.5 reduce-scatter.4
where the time goes:
time: 599 us
  waiting for transfers between devices  493 us (82%)
  local copies, waits for them, and re-layouts  38.6 us (6%)
  matrix products  35.5 us (6%)
  other arithmetic  15.4 us (3%)
  between operations  13.8 us (2%)
    reduce_scatter x1, waiting for transfers between devices, local(): lax.psum_scatter(lax.dot_general(token_slots, grads_buffer, ROWS_CONTRACT...  235 us
    unnamed x6, waiting for transfers between devices  75 us
    all_gather x1, waiting for transfers between devices, local(): lax.all_gather(up_weight, 'dp', axis=0, tiled=True)  67.5 us
    all_gather x1, waiting for transfers between devices, local(): lax.all_gather(down_weight_t, 'dp', axis=0, tiled=True)  60.4 us
    all_gather x1, waiting for transfers between devices, local(): lax.all_gather(gate_weight, 'dp', axis=0, tiled=True)  54.7 us
  transfers between devices with their start and end apart: 5, of which 5 were waited for; matrix products, arithmetic and copies ran while one was open for 6% of the time, Pallas kernels for 0%

commit v1 on v0

v1 whole, which is shorter than its diff:
```python
import functools

import jax
import jax.numpy as jnp
from jax import lax
from jax.experimental import pallas as pl
from jax.experimental.pallas import tpu as pltpu
from jax.sharding import PartitionSpec as P

BLOCK = 128
MESH = pl.DeviceIdType.MESH
Z, X, Y, C = 4, 2, 2, 2
HALVES = 2
PIECES = 3 * HALVES
X_FIRST = (0,)
RIGHT, LEFT, ACROSS = 0, 1, 2


def kernel(
    scale,
    tokens_hbm, cotangent_hbm, routes_ref, gates_ref, count_ref, gate_hbm, up_hbm, down_hbm,
    grad_tokens_ref, grad_gate_ref, grad_up_ref,
    tokens, cotangent, panel, flipped, gate_acc, up_acc, back_acc, grads, row_gate,
    own_sum, cross_out, cross_in, right_sum, left_sum, share_out, share_in,
    load_sem, gather_send, gather_recv, cross_send, cross_recv,
    line_send, line_recv, share_send, share_recv,
):
    dp, expert = lax.axis_index("dp"), lax.axis_index("expert")
    z, x = dp // X, dp % X
    y, c = expert // C, expert % C
    other_x = 1 - x
    weights = (gate_hbm, up_hbm, down_hbm)
    shard_rows, width = gate_hbm.shape
    piece_rows = shard_rows // HALVES
    pair_rows = X * shard_rows
    row_count = tokens.shape[0]

    across = (z * X + other_x, expert)
    targets = {RIGHT: (dp + X, expert), LEFT: (dp - X, expert), ACROSS: across}
    has = {RIGHT: z < Z - 1, LEFT: z > 0}

    def when(direction, fn):
        if direction == ACROSS:
            fn()
        else:
            pl.when(has[direction])(fn)

    share_targets = []
    for j in range(1, Y * C):
        y_to = 1 - y if j // C else y
        c_to = 1 - c if j % C else c
        share_targets.append(y_to * C + c_to)

    barrier = pltpu.get_barrier_semaphore()
    for direction in (RIGHT, LEFT, ACROSS):
        when(direction, lambda direction=direction: pl.semaphore_signal(
            barrier, inc=1, device_id=targets[direction], device_id_type=MESH))
    for to in share_targets:
        pl.semaphore_signal(barrier, inc=1, device_id=(dp, to), device_id_type=MESH)
    pl.semaphore_wait(barrier, 5 + z * (Z - 1 - z) // 2)

    def piece(k, p):
        start = pl.multiple_of(p * shard_rows + (k % HALVES) * piece_rows, 16)
        return panel.at[k // HALVES, pl.ds(start, piece_rows), :]

    def gather_copy(direction, k, p, own=False):
        if own:
            source = weights[k // HALVES].at[pl.ds((k % HALVES) * piece_rows, piece_rows), :]
        else:
            source = piece(k, p)
        return pltpu.make_async_remote_copy(
            src_ref=source, dst_ref=piece(k, p),
            send_sem=gather_send.at[direction, p, k], recv_sem=gather_recv.at[p, k],
            device_id=targets[direction], device_id_type=MESH,
        )

    def gather_send_piece(direction, k, p, own=False):
        when(direction, lambda: gather_copy(direction, k, p, own).start())

    def gather_wait(k, p):
        gather_copy(ACROSS, k, p).wait_recv()

    mine, facing = dp, z * X + other_x
    for k in range(PIECES):
        for direction in (ACROSS, RIGHT, LEFT):
            gather_send_piece(direction, k, mine, own=True)

    loads = []
    for t in range(3):
        rows = pl.ds(pl.multiple_of(mine * shard_rows, 16), shard_rows)
        loads.append(pltpu.make_async_copy(weights[t], panel.at[t, rows, :], load_sem.at[t]))
    loads.append(pltpu.make_async_copy(tokens_hbm, tokens, load_sem.at[3]))
    loads.append(pltpu.make_async_copy(cotangent_hbm, cotangent, load_sem.at[4]))
    for load in loads:
        load.start()

    slots = lax.broadcasted_iota(jnp.int32, (1, row_count), 1)
    live_gate = jnp.where(slots // BLOCK < count_ref[0], gates_ref[...], 0.0)
    rows_here = lax.broadcasted_iota(jnp.int32, (row_count, 1), 0)
    row_gate[...] = jnp.sum(
        jnp.where(rows_here == routes_ref[...], live_gate, 0.0), axis=1, keepdims=True)
    for acc in (gate_acc, up_acc, back_acc):
        acc[...] = jnp.zeros_like(acc)
    for load in loads:
        load.wait()

    @pl.loop(0, tokens.shape[1] // 128)
    def _(i):
        columns = pl.ds(pl.multiple_of(i * 128, 128), 128)
        flipped[columns, :] = tokens[:, columns].T

    def project(at):
        for k in range(PIECES):
            if k not in X_FIRST:
                gather_wait(k, at * X + other_x)
        span = pl.ds(pl.multiple_of(at * pair_rows, 128), pair_rows)
        for t, (acc, rows) in enumerate(
            ((gate_acc, tokens), (up_acc, tokens), (back_acc, cotangent))
        ):
            acc[...] += jnp.dot(rows[:, span], panel[t, span, :], preferred_element_type=jnp.float32)

    for k in X_FIRST:
        gather_wait(k, facing)
        for direction in (RIGHT, LEFT):
            gather_send_piece(direction, k, facing)

    def arrivals(distance, k):
        for came, onward, exists in (
            (z - distance, RIGHT, z >= distance), (z + distance, LEFT, z + distance < Z)
        ):
            @pl.when(exists)
            def _(came=came, onward=onward):
                gather_wait(k, came * X + x)
                gather_send_piece(onward, k, came * X + x)
                if k in X_FIRST:
                    gather_wait(k, came * X + other_x)
                    gather_send_piece(onward, k, came * X + other_x)
                else:
                    gather_send_piece(ACROSS, k, came * X + x)

    for distance in range(1, Z):
        for k in range(PIECES):
            arrivals(distance, k)
        if distance == 1:
            project(z)
        else:
            pl.when(z >= distance - 1)(lambda: project(z - distance + 1))
            pl.when(z + distance - 1 < Z)(lambda: project(z + distance - 1))
    pl.when(z == Z - 1)(lambda: project(z - (Z - 1)))
    pl.when(z == 0)(lambda: project(z + Z - 1))

    @pl.loop(0, row_count // 64)
    def _(i):
        rows = pl.ds(pl.multiple_of(i * 64, 64), 64)
        gate_val, up_val = gate_acc[rows, :], up_acc[rows, :]
        hidden_grad = row_gate[rows, :] * back_acc[rows, :]
        gate_sigmoid = jax.nn.sigmoid(gate_val)
        grads[1, rows, :] = (hidden_grad * (gate_val * gate_sigmoid)).astype(jnp.bfloat16)
        grads[0, rows, :] = (
            hidden_grad * up_val * gate_sigmoid * (1.0 + gate_val * (1.0 - gate_sigmoid))
        ).astype(jnp.bfloat16)

    def weight_term(at_z, at_x, t):
        start = pl.multiple_of((at_z * X + at_x) * shard_rows, 16)
        return jnp.dot(
            flipped[pl.ds(start, shard_rows), :], grads[t], preferred_element_type=jnp.float32)

    def cross_copy(at, t):
        return pltpu.make_async_remote_copy(
            src_ref=cross_out.at[at, t], dst_ref=cross_in.at[at, t],
            send_sem=cross_send.at[at, t], recv_sem=cross_recv.at[at, t],
            device_id=across, device_id_type=MESH,
        )

    order = (3 * (1 - z // 2), 2 - 2 * z + 5 * (z // 2), 1 + z % 2, z)
    for at in order:
        for t in range(2):
            cross_out[at, t] = weight_term(at, other_x, t).astype(jnp.bfloat16)
            cross_copy(at, t).start()

    def share_copy(j):
        return pltpu.make_async_remote_copy(
            src_ref=share_out.at[j], dst_ref=share_in.at[j],
            send_sem=share_send.at[j], recv_sem=share_recv.at[j],
            device_id=(dp, share_targets[j]), device_id_type=MESH,
        )

    def share_term(to):
        span = pl.ds(pl.multiple_of(to * pair_rows, 16), pair_rows)
        total = None
        for t in range(2):
            term = lax.dot_general(
                grads[t], panel[t, span, :], (((1,), (1,)), ((), ())),
                preferred_element_type=jnp.float32)
            total = term if total is None else total + term
        return total.astype(jnp.bfloat16)

    for j, to in enumerate(share_targets):
        share_out[j] = share_term(to)
        share_copy(j).start()

    @pl.loop(0, Z)
    def _(at):
        for t in range(2):
            own_sum[at, t] = weight_term(at, x, t)

    share_out[Y * C - 1] = share_term(expert)

    sums = {RIGHT: right_sum, LEFT: left_sum}
    upstream = {RIGHT: has[LEFT], LEFT: has[RIGHT]}

    def line_copy(direction, at, t):
        return pltpu.make_async_remote_copy(
            src_ref=sums[direction].at[at, t], dst_ref=sums[direction].at[at, t],
            send_sem=line_send.at[direction, at, t], recv_sem=line_recv.at[direction, at, t],
            device_id=targets[direction], device_id_type=MESH,
        )

    def chunks(fn):
        @pl.loop(0, shard_rows // 64)
        def _(i):
            fn(pl.ds(pl.multiple_of(i * 64, 64), 64))

    def line_step(direction, at):
        for t in range(2):
            cross_copy(at, t).wait_recv()
            def start(rows):
                sums[direction][at, t, rows, :] = (
                    own_sum[at, t, rows, :] + cross_in[at, t, rows, :].astype(jnp.float32)
                ).astype(jnp.bfloat16)
            def add(rows):
                sums[direction][at, t, rows, :] = (
                    own_sum[at, t, rows, :] + cross_in[at, t, rows, :].astype(jnp.float32)
                    + sums[direction][at, t, rows, :].astype(jnp.float32)
                ).astype(jnp.bfloat16)

            @pl.when(upstream[direction])
            def _():
                line_copy(direction, at, t).wait_recv()
                chunks(add)

            @pl.when(jnp.logical_not(upstream[direction]))
            def _():
                chunks(start)

            line_copy(direction, at, t).start()

    for j in range(Z - 1):
        pl.when(z < Z - 1 - j)(lambda: line_step(RIGHT, Z - 1 - j))
        pl.when(z > j)(lambda: line_step(LEFT, j))

    for j in range(Y * C - 1):
        share_copy(j).wait_recv()

    @pl.loop(0, row_count // 64)
    def _(i):
        rows = pl.ds(pl.multiple_of(i * 64, 64), 64)
        total = share_out[Y * C - 1, rows, :].astype(jnp.float32)
        for j in range(Y * C - 1):
            total = total + share_in[j, rows, :].astype(jnp.float32)
        grad_tokens_ref[rows, :] = total.astype(jnp.bfloat16)

    for t, out in enumerate((grad_gate_ref, grad_up_ref)):
        cross_copy(z, t).wait_recv()

        def base(rows):
            own_sum[z, t, rows, :] += cross_in[z, t, rows, :].astype(jnp.float32)
        chunks(base)
        for direction in (RIGHT, LEFT):
            @pl.when(upstream[direction])
            def _():
                line_copy(direction, z, t).wait_recv()
                def add(rows):
                    own_sum[z, t, rows, :] += sums[direction][z, t, rows, :].astype(jnp.float32)
                chunks(add)
        def finish(rows):
            out[rows, :] = own_sum[z, t, rows, :] * scale
        chunks(finish)

    for k in range(PIECES):
        for direction in (ACROSS, RIGHT, LEFT):
            when(direction, lambda: gather_copy(direction, k, mine, own=True).wait_send())
        if k in X_FIRST:
            for direction in (RIGHT, LEFT):
                when(direction, lambda: gather_copy(direction, k, facing).wait_send())
        for distance in range(1, Z):
            for came, onward, exists in (
                (z - distance, RIGHT, z >= distance), (z + distance, LEFT, z + distance < Z)
            ):
                @pl.when(exists)
                def _(came=came, onward=onward):
                    when(onward, lambda: gather_copy(onward, k, came * X + x).wait_send())
                    if k in X_FIRST:
                        when(onward, lambda: gather_copy(onward, k, came * X + other_x).wait_send())
                    else:
                        gather_copy(ACROSS, k, came * X + x).wait_send()
    for t in range(2):
        for at in range(Z):
            cross_copy(at, t).wait_send()
        for at in range(Z):
            pl.when(at > z)(lambda: line_copy(RIGHT, at, t).wait_send())
            pl.when(at < z)(lambda: line_copy(LEFT, at, t).wait_send())
    for j in range(Y * C - 1):
        share_copy(j).wait_send()


def local_kernel(
    tokens, grad_out, route_rows, route_gate, block_count, gate_weight, up_weight, down_weight_t
):
    row_count, features = tokens.shape
    shard_rows, width = gate_weight.shape
    scale = float(lax.axis_size("dp") * row_count) ** (-0.5)
    pair_rows = X * shard_rows
    bf16, f32 = jnp.bfloat16, jnp.float32
    anywhere, vmem = pl.BlockSpec(memory_space=pl.ANY), pl.BlockSpec(memory_space=pltpu.VMEM)
    dma = pltpu.SemaphoreType.DMA
    flops = 2 * row_count * features * width * 7
    return pl.pallas_call(
        functools.partial(kernel, scale),
        out_shape=(
            jax.ShapeDtypeStruct((row_count, pair_rows), bf16),
            jax.ShapeDtypeStruct((shard_rows, width), f32),
            jax.ShapeDtypeStruct((shard_rows, width), f32),
        ),
        in_specs=[
            anywhere, anywhere, vmem, vmem, pl.BlockSpec(memory_space=pltpu.SMEM),
            anywhere, anywhere, anywhere,
        ],
        out_specs=(vmem, vmem, vmem),
        scratch_shapes=[
            pltpu.VMEM((row_count, features), bf16),
            pltpu.VMEM((row_count, features), bf16),
            pltpu.VMEM((3, features, width), bf16),
            pltpu.VMEM((features, row_count), bf16),
            pltpu.VMEM((row_count, width), f32),
            pltpu.VMEM((row_count, width), f32),
            pltpu.VMEM((row_count, width), f32),
            pltpu.VMEM((2, row_count, width), bf16),
            pltpu.VMEM((row_count, 1), f32),
            pltpu.VMEM((Z, 2, shard_rows, width), f32),
            pltpu.VMEM((Z, 2, shard_rows, width), bf16),
            pltpu.VMEM((Z, 2, shard_rows, width), bf16),
            pltpu.VMEM((Z, 2, shard_rows, width), bf16),
            pltpu.VMEM((Z, 2, shard_rows, width), bf16),
            pltpu.VMEM((Y * C, row_count, pair_rows), bf16),
            pltpu.VMEM((Y * C - 1, row_count, pair_rows), bf16),
            dma((5,)),
            dma((3, Z * X, PIECES)), dma((Z * X, PIECES)),
            dma((Z, 2)), dma((Z, 2)),
            dma((2, Z, 2)), dma((2, Z, 2)),
            dma((Y * C - 1,)), dma((Y * C - 1,)),
        ],
        compiler_params=pltpu.CompilerParams(
            collective_id=0, has_side_effects=True, vmem_limit_bytes=62 * 1024 * 1024
        ),
        cost_estimate=pl.CostEstimate(flops=flops, bytes_accessed=16 * 2**20, transcendentals=0),
    )(
        tokens, grad_out, route_rows.reshape(1, -1), route_gate.reshape(1, -1), block_count,
        gate_weight, up_weight, down_weight_t,
    )


def local_plain(
    tokens, grad_out, route_rows, route_gate, block_count, gate_weight, up_weight, down_weight_t
):
    row_count = tokens.shape[0]
    width = gate_weight.shape[1]
    gate_panel, up_panel, down_panel = (
        lax.all_gather(weight, "dp", axis=0, tiled=True)
        for weight in (gate_weight, up_weight, down_weight_t)
    )
    both_panels = jnp.concatenate([gate_panel, up_panel], axis=1)
    live = jnp.arange(row_count) // BLOCK < block_count[0]
    live_gate = jnp.zeros_like(route_gate).at[route_rows].set(jnp.where(live, route_gate, 0.0))
    projected = jnp.dot(tokens, both_panels, preferred_element_type=jnp.float32)
    gate_val, up_val = projected[:, :width], projected[:, width:]
    back = jnp.dot(grad_out, down_panel, preferred_element_type=jnp.float32)
    hidden_grad = live_gate[:, None] * back
    gate_sigmoid = jax.nn.sigmoid(gate_val)
    grad_up = hidden_grad * (gate_val * gate_sigmoid)
    grad_gate = hidden_grad * up_val * gate_sigmoid * (1.0 + gate_val * (1.0 - gate_sigmoid))
    grads = jnp.concatenate([grad_gate, grad_up], axis=1).astype(jnp.bfloat16)
    partial = lax.dot_general(
        grads, both_panels, (((1,), (1,)), ((), ())), preferred_element_type=jnp.float32)
    grad_tokens = lax.psum_scatter(
        partial.astype(jnp.bfloat16), "expert", scatter_dimension=1, tiled=True)
    weight_share = lax.psum_scatter(
        lax.dot_general(
            tokens, grads, (((0,), (0,)), ((), ())), preferred_element_type=jnp.float32),
        "dp", scatter_dimension=0, tiled=True)
    weight_share = weight_share * float(lax.axis_size("dp") * row_count) ** (-0.5)
    return grad_tokens, weight_share[:, :width], weight_share[:, width:]


def solution(mesh):
    by_dp, both = P("dp"), P("dp", "expert")
    in_specs = (P("dp", None), P("dp", None), by_dp, by_dp, by_dp, both, both, both)
    small = (mesh.shape["dp"], mesh.shape["expert"]) == (Z * X, Y * C)
    return jax.shard_map(
        local_kernel if small else local_plain,
        mesh=mesh, in_specs=in_specs, out_specs=(both, both, both), check_vma=False)
```

time: 599 us -> 210 us (0.35)
  waiting for transfers between devices: 493 us -> 0 us
  Pallas kernels: 0 us -> 203 us
  matrix products: 35.5 us -> 0 us
  local copies, waits for them, and re-layouts: 38.6 us -> 5.34 us
  other arithmetic: 15.4 us -> 0 us
  between operations: 13.8 us -> 1.3 us
    reduce_scatter x1 -> x0, waiting for transfers between devices: 235 us -> none  [local(): lax.psum_scatter(lax.dot_general(token_slots, grads_buffer, ROWS_CONTRACT...]
    pallas_call x0 -> x1, Pallas kernels: none -> 203 us  [local_kernel(): pl.pallas_call(functools.partial(kernel, scale), out_shape=(jax.ShapeDtyp...]
    all_gather x3 -> x0, waiting for transfers between devices: 183 us -> none  [the longest x1 67.5 us: local(): lax.all_gather(up_weight, 'dp', axis=0, tiled=True)]
    unnamed x6 -> x0, waiting for transfers between devices: 75 us -> none
    dot_general x7 -> x0, matrix products: 35.5 us -> none  [the longest x2 11.4 us: input_block(): lax.dot_general(grads_block, both_panels, COLS_CONTRACT, preferred_elemen...]
    gather x3 -> x0, local copies, waits for them, and re-layouts: 19.5 us -> none  [the longest x1 10.4 us: local(): token_slots = jnp.take(tokens, route_rows, axis=0)]
    concatenate x1 -> x0, other arithmetic: 7.12 us -> none  [local(): both_panels = jnp.concatenate([gate_panel, up_panel], axis=1)]
  transfers between devices with their start and end apart: 5 -> 0, of which waited for: 5 -> 0; matrix products, arithmetic and copies ran while one was open for 6% -> 0% of each run, Pallas kernels for 0% -> 0%
where the time goes in v1:
time: 210 us
  Pallas kernels  203 us (97%)
  local copies, waits for them, and re-layouts  5.34 us (3%)
    pallas_call x1, Pallas kernels, local_kernel(): pl.pallas_call(functools.partial(kernel, scale), out_shape=(jax.ShapeDtyp...  203 us
    unnamed x5, local copies, waits for them, and re-layouts  5.34 us

profile of v1, /device:TPU:0, one launch (start us, length us, event | category | flops | bytes accessed | tf_op | source)
XLA Modules:
  0.0 210.1 jit_solution(1281801950269815640)
XLA Ops:
  1.3 203.4 %shard_map.103 = (bf16[512,896]{1,0:T(8,128)(2,1)}, f32[448,512]{1,0:T(8,128)}, f32[448,512]{1,0:T(8,128)}) custom-call(bf16[512,3584]{1,0:T(8,128)(2,1)} %tokens_hbm.1, bf16[512,3584]{1,0:T(8,128)(2,1)} %cotangent_hbm.1, s32[1,512]{1,0:T(1,128)} %bitcast.2, f32[1,512]{1,0:T(1,128)} %bitcast.3, s32[1]{0:T(128)S(6)} %copy.14.count_ref, ...), custom_call_target="tpu_custom_call" | custom-call | flops 13153337344 | bytes 16777216 | tf_op jit(solution)/shard_map/pallas_call | solution.py:318
  204.7 0.0 copy-start
  204.7 2.3 %copy.15 = bf16[512,896]{1,0:T(8,128)(2,1)} copy(bf16[512,896]{1,0:T(8,128)(2,1)} %get-tuple-element.6) | data formatting | bytes 1835008
  207.0 2.2 %copy.16 = f32[448,512]{1,0:T(8,128)} copy(f32[448,512]{1,0:T(8,128)} %get-tuple-element.7) | data formatting | bytes 1835008
  209.1 0.0 copy-done
  209.2 0.9 copy.17
Async XLA Ops:
  204.7 4.4 %copy-start = (f32[448,512]{1,0:T(8,128)S(1)}, f32[448,512]{1,0:T(8,128)}, u32[]{:S(2)}) copy-start(f32[448,512]{1,0:T(8,128)} %get-tuple-element.8) | copy-start | bytes 2752516

commit v2 on v1

--- a/solution.py
+++ b/solution.py
@@ -12,7 +12,7 @@
 Z, X, Y, C = 4, 2, 2, 2
 HALVES = 2
 PIECES = 3 * HALVES
-X_FIRST = (0,)
+X_FIRST = (0, 3, 4)
 RIGHT, LEFT, ACROSS = 0, 1, 2
 
 
@@ -31,7 +31,7 @@
     other_x = 1 - x
     weights = (gate_hbm, up_hbm, down_hbm)
     shard_rows, width = gate_hbm.shape
-    piece_rows = shard_rows // HALVES
+    half_width = width // HALVES
     pair_rows = X * shard_rows
     row_count = tokens.shape[0]
 
@@ -60,12 +60,12 @@
     pl.semaphore_wait(barrier, 5 + z * (Z - 1 - z) // 2)
 
     def piece(k, p):
-        start = pl.multiple_of(p * shard_rows + (k % HALVES) * piece_rows, 16)
-        return panel.at[k // HALVES, pl.ds(start, piece_rows), :]
+        start = pl.multiple_of(p * shard_rows, 16)
+        return panel.at[k // 3, k % 3, pl.ds(start, shard_rows), :]
 
     def gather_copy(direction, k, p, own=False):
         if own:
-            source = weights[k // HALVES].at[pl.ds((k % HALVES) * piece_rows, piece_rows), :]
+            source = weights[k % 3].at[:, pl.ds(k // 3 * half_width, half_width)]
         else:
             source = piece(k, p)
         return pltpu.make_async_remote_copy(
@@ -81,16 +81,17 @@
         gather_copy(ACROSS, k, p).wait_recv()
 
     mine, facing = dp, z * X + other_x
-    for k in range(PIECES):
+    for k in range(3):
         for direction in (ACROSS, RIGHT, LEFT):
             gather_send_piece(direction, k, mine, own=True)
 
     loads = []
-    for t in range(3):
-        rows = pl.ds(pl.multiple_of(mine * shard_rows, 16), shard_rows)
-        loads.append(pltpu.make_async_copy(weights[t], panel.at[t, rows, :], load_sem.at[t]))
-    loads.append(pltpu.make_async_copy(tokens_hbm, tokens, load_sem.at[3]))
-    loads.append(pltpu.make_async_copy(cotangent_hbm, cotangent, load_sem.at[4]))
+    for k in range(PIECES):
+        columns = pl.ds(k // 3 * half_width, half_width)
+        loads.append(pltpu.make_async_copy(
+            weights[k % 3].at[:, columns], piece(k, mine), load_sem.at[k]))
+    loads.append(pltpu.make_async_copy(tokens_hbm, tokens, load_sem.at[PIECES]))
+    loads.append(pltpu.make_async_copy(cotangent_hbm, cotangent, load_sem.at[PIECES + 1]))
     for load in loads:
         load.start()
 
@@ -99,8 +100,6 @@
     rows_here = lax.broadcasted_iota(jnp.int32, (row_count, 1), 0)
     row_gate[...] = jnp.sum(
         jnp.where(rows_here == routes_ref[...], live_gate, 0.0), axis=1, keepdims=True)
-    for acc in (gate_acc, up_acc, back_acc):
-        acc[...] = jnp.zeros_like(acc)
     for load in loads:
         load.wait()
 
@@ -109,17 +108,18 @@
         columns = pl.ds(pl.multiple_of(i * 128, 128), 128)
         flipped[columns, :] = tokens[:, columns].T
 
-    def project(at):
-        for k in range(PIECES):
+    def project(at, half):
+        for k in range(half * 3, half * 3 + 3):
             if k not in X_FIRST:
                 gather_wait(k, at * X + other_x)
         span = pl.ds(pl.multiple_of(at * pair_rows, 128), pair_rows)
         for t, (acc, rows) in enumerate(
             ((gate_acc, tokens), (up_acc, tokens), (back_acc, cotangent))
         ):
-            acc[...] += jnp.dot(rows[:, span], panel[t, span, :], preferred_element_type=jnp.float32)
-
-    for k in X_FIRST:
+            acc[...] += jnp.dot(
+                rows[:, span], panel[half, t, span, :], preferred_element_type=jnp.float32)
+
+    def pass_facing(k):
         gather_wait(k, facing)
         for direction in (RIGHT, LEFT):
             gather_send_piece(direction, k, facing)
@@ -138,27 +138,18 @@
                 else:
                     gather_send_piece(ACROSS, k, came * X + x)
 
-    for distance in range(1, Z):
-        for k in range(PIECES):
-            arrivals(distance, k)
-        if distance == 1:
-            project(z)
-        else:
-            pl.when(z >= distance - 1)(lambda: project(z - distance + 1))
-            pl.when(z + distance - 1 < Z)(lambda: project(z + distance - 1))
-    pl.when(z == Z - 1)(lambda: project(z - (Z - 1)))
-    pl.when(z == 0)(lambda: project(z + Z - 1))
-
-    @pl.loop(0, row_count // 64)
-    def _(i):
-        rows = pl.ds(pl.multiple_of(i * 64, 64), 64)
-        gate_val, up_val = gate_acc[rows, :], up_acc[rows, :]
-        hidden_grad = row_gate[rows, :] * back_acc[rows, :]
-        gate_sigmoid = jax.nn.sigmoid(gate_val)
-        grads[1, rows, :] = (hidden_grad * (gate_val * gate_sigmoid)).astype(jnp.bfloat16)
-        grads[0, rows, :] = (
-            hidden_grad * up_val * gate_sigmoid * (1.0 + gate_val * (1.0 - gate_sigmoid))
-        ).astype(jnp.bfloat16)
+    def hidden_gradients(half):
+        @pl.loop(0, row_count // 64)
+        def _(i):
+            rows = pl.ds(pl.multiple_of(i * 64, 64), 64)
+            gate_val, up_val = gate_acc[rows, :], up_acc[rows, :]
+            hidden_grad = row_gate[rows, :] * back_acc[rows, :]
+            gate_sigmoid = jax.nn.sigmoid(gate_val)
+            grads[half, rows, half_width:] = (
+                hidden_grad * (gate_val * gate_sigmoid)).astype(jnp.bfloat16)
+            grads[half, rows, :half_width] = (
+                hidden_grad * up_val * gate_sigmoid * (1.0 + gate_val * (1.0 - gate_sigmoid))
+            ).astype(jnp.bfloat16)
 
     def weight_term(at_z, at_x, t):
         start = pl.multiple_of((at_z * X + at_x) * shard_rows, 16)
@@ -173,10 +164,15 @@
         )
 
     order = (3 * (1 - z // 2), 2 - 2 * z + 5 * (z // 2), 1 + z % 2, z)
-    for at in order:
-        for t in range(2):
+    def send_terms(t):
+        for at in order:
             cross_out[at, t] = weight_term(at, other_x, t).astype(jnp.bfloat16)
             cross_copy(at, t).start()
+
+    def keep_terms(t):
+        @pl.loop(0, Z)
+        def _(at):
+            own_sum[at, t] = weight_term(at, x, t)
 
     def share_copy(j):
         return pltpu.make_async_remote_copy(
@@ -188,23 +184,13 @@
     def share_term(to):
         span = pl.ds(pl.multiple_of(to * pair_rows, 16), pair_rows)
         total = None
-        for t in range(2):
-            term = lax.dot_general(
-                grads[t], panel[t, span, :], (((1,), (1,)), ((), ())),
-                preferred_element_type=jnp.float32)
-            total = term if total is None else total + term
+        for half in range(HALVES):
+            for t in range(2):
+                term = lax.dot_general(
+                    grads[half, :, t * half_width:(t + 1) * half_width], panel[half, t, span, :],
+                    (((1,), (1,)), ((), ())), preferred_element_type=jnp.float32)
+                total = term if total is None else total + term
         return total.astype(jnp.bfloat16)
-
-    for j, to in enumerate(share_targets):
-        share_out[j] = share_term(to)
-        share_copy(j).start()
-
-    @pl.loop(0, Z)
-    def _(at):
-        for t in range(2):
-            own_sum[at, t] = weight_term(at, x, t)
-
-    share_out[Y * C - 1] = share_term(expert)
 
     sums = {RIGHT: right_sum, LEFT: left_sum}
     upstream = {RIGHT: has[LEFT], LEFT: has[RIGHT]}
@@ -221,33 +207,75 @@
         def _(i):
             fn(pl.ds(pl.multiple_of(i * 64, 64), 64))
 
-    def line_step(direction, at):
-        for t in range(2):
-            cross_copy(at, t).wait_recv()
-            def start(rows):
-                sums[direction][at, t, rows, :] = (
-                    own_sum[at, t, rows, :] + cross_in[at, t, rows, :].astype(jnp.float32)
-                ).astype(jnp.bfloat16)
-            def add(rows):
-                sums[direction][at, t, rows, :] = (
-                    own_sum[at, t, rows, :] + cross_in[at, t, rows, :].astype(jnp.float32)
-                    + sums[direction][at, t, rows, :].astype(jnp.float32)
-                ).astype(jnp.bfloat16)
-
-            @pl.when(upstream[direction])
-            def _():
-                line_copy(direction, at, t).wait_recv()
-                chunks(add)
-
-            @pl.when(jnp.logical_not(upstream[direction]))
-            def _():
-                chunks(start)
-
-            line_copy(direction, at, t).start()
-
+    def line_step(direction, at, t):
+        cross_copy(at, t).wait_recv()
+
+        def start(rows):
+            sums[direction][at, t, rows, :] = (
+                own_sum[at, t, rows, :] + cross_in[at, t, rows, :].astype(jnp.float32)
+            ).astype(jnp.bfloat16)
+
+        def add(rows):
+            sums[direction][at, t, rows, :] = (
+                own_sum[at, t, rows, :] + cross_in[at, t, rows, :].astype(jnp.float32)
+                + sums[direction][at, t, rows, :].astype(jnp.float32)
+            ).astype(jnp.bfloat16)
+
+        @pl.when(upstream[direction])
+        def _():
+            line_copy(direction, at, t).wait_recv()
+            chunks(add)
+
+        @pl.when(jnp.logical_not(upstream[direction]))
+        def _():
+            chunks(start)
+
+        line_copy(direction, at, t).start()
+
+    def line_round(j, t):
+        pl.when(z < Z - 1 - j)(lambda: line_step(RIGHT, Z - 1 - j, t))
+        pl.when(z > j)(lambda: line_step(LEFT, j, t))
+
+    for half in range(HALVES):
+        pieces = range(half * 3, half * 3 + 3)
+        for acc in (gate_acc, up_acc, back_acc):
+            acc[...] = jnp.zeros_like(acc)
+        if half == 0:
+            pass_facing(0)
+        for distance in range(1, Z):
+            for k in pieces:
+                arrivals(distance, k)
+            if half == 0 and distance == 2:
+                for k in range(3, PIECES):
+                    for direction in (ACROSS, RIGHT, LEFT):
+                        if k in X_FIRST or direction != ACROSS:
+                            gather_send_piece(direction, k, mine, own=True)
+            if half == 0 and distance == 3:
+                for k in range(3, PIECES):
+                    if k in X_FIRST:
+                        pass_facing(k)
+                    else:
+                        gather_send_piece(ACROSS, k, mine, own=True)
+            if distance == 1:
+                project(z, half)
+            else:
+                pl.when(z >= distance - 1)(lambda: project(z - distance + 1, half))
+                pl.when(z + distance - 1 < Z)(lambda: project(z + distance - 1, half))
+            if half == 1:
+                line_round(distance - 1, 0)
+        pl.when(z == Z - 1)(lambda: project(z - (Z - 1), half))
+        pl.when(z == 0)(lambda: project(z + Z - 1, half))
+        hidden_gradients(half)
+        send_terms(half)
+        if half == 1:
+            for j, to in enumerate(share_targets):
+                share_out[j] = share_term(to)
+                share_copy(j).start()
+        keep_terms(half)
+
+    share_out[Y * C - 1] = share_term(expert)
     for j in range(Z - 1):
-        pl.when(z < Z - 1 - j)(lambda: line_step(RIGHT, Z - 1 - j))
-        pl.when(z > j)(lambda: line_step(LEFT, j))
+        line_round(j, 1)
 
     for j in range(Y * C - 1):
         share_copy(j).wait_recv()
@@ -260,7 +288,7 @@
             total = total + share_in[j, rows, :].astype(jnp.float32)
         grad_tokens_ref[rows, :] = total.astype(jnp.bfloat16)
 
-    for t, out in enumerate((grad_gate_ref, grad_up_ref)):
+    for t in range(HALVES):
         cross_copy(z, t).wait_recv()
 
         def base(rows):
@@ -274,7 +302,9 @@
                     own_sum[z, t, rows, :] += sums[direction][z, t, rows, :].astype(jnp.float32)
                 chunks(add)
         def finish(rows):
-            out[rows, :] = own_sum[z, t, rows, :] * scale
+            columns = pl.ds(t * half_width, half_width)
+            grad_gate_ref[rows, columns] = own_sum[z, t, rows, :half_width] * scale
+            grad_up_ref[rows, columns] = own_sum[z, t, rows, half_width:] * scale
         chunks(finish)
 
     for k in range(PIECES):
@@ -330,11 +360,11 @@
         scratch_shapes=[
             pltpu.VMEM((row_count, features), bf16),
             pltpu.VMEM((row_count, features), bf16),
-            pltpu.VMEM((3, features, width), bf16),
+            pltpu.VMEM((HALVES, 3, features, width // HALVES), bf16),
             pltpu.VMEM((features, row_count), bf16),
-            pltpu.VMEM((row_count, width), f32),
-            pltpu.VMEM((row_count, width), f32),
-            pltpu.VMEM((row_count, width), f32),
+            pltpu.VMEM((row_count, width // HALVES), f32),
+            pltpu.VMEM((row_count, width // HALVES), f32),
+            pltpu.VMEM((row_count, width // HALVES), f32),
             pltpu.VMEM((2, row_count, width), bf16),
             pltpu.VMEM((row_count, 1), f32),
             pltpu.VMEM((Z, 2, shard_rows, width), f32),
@@ -344,7 +374,7 @@
             pltpu.VMEM((Z, 2, shard_rows, width), bf16),
             pltpu.VMEM((Y * C, row_count, pair_rows), bf16),
             pltpu.VMEM((Y * C - 1, row_count, pair_rows), bf16),
-            dma((5,)),
+            dma((PIECES + 2,)),
             dma((3, Z * X, PIECES)), dma((Z * X, PIECES)),
             dma((Z, 2)), dma((Z, 2)),
             dma((2, Z, 2)), dma((2, Z, 2)),

time: 210 us -> 223 us (1.062)
  Pallas kernels: 203 us -> 216 us
    pallas_call x1, Pallas kernels: 203 us -> 216 us  [local_kernel(): pl.pallas_call(functools.partial(kernel, scale), out_shape=(jax.ShapeDtyp...]
where the time goes in v2:
time: 223 us
  Pallas kernels  216 us (97%)
  local copies, waits for them, and re-layouts  5.34 us (2%)
    pallas_call x1, Pallas kernels, local_kernel(): pl.pallas_call(functools.partial(kernel, scale), out_shape=(jax.ShapeDtyp...  216 us
    unnamed x5, local copies, waits for them, and re-layouts  5.34 us

profile of v2, /device:TPU:0, one launch (start us, length us, event | category | flops | bytes accessed | tf_op | source)
XLA Modules:
  0.0 222.8 jit_solution(3615745137580303435)
XLA Ops:
  1.3 216.2 %shard_map.103 = (bf16[512,896]{1,0:T(8,128)(2,1)}, f32[448,512]{1,0:T(8,128)}, f32[448,512]{1,0:T(8,128)}) custom-call(bf16[512,3584]{1,0:T(8,128)(2,1)} %tokens_hbm.1, bf16[512,3584]{1,0:T(8,128)(2,1)} %cotangent_hbm.1, s32[1,512]{1,0:T(1,128)} %bitcast.2, f32[1,512]{1,0:T(1,128)} %bitcast.3, s32[1]{0:T(128)S(6)} %copy.14.count_ref, ...), custom_call_target="tpu_custom_call" | custom-call | flops 13153337344 | bytes 16777216 | tf_op jit(solution)/shard_map/pallas_call | solution.py:348
  217.5 0.0 copy-start
  217.5 2.3 %copy.15 = bf16[512,896]{1,0:T(8,128)(2,1)} copy(bf16[512,896]{1,0:T(8,128)(2,1)} %get-tuple-element.6) | data formatting | bytes 1835008
  219.8 2.2 copy.16
  221.9 0.0 copy-done
  221.9 0.9 copy.17
Async XLA Ops:
  217.5 4.4 %copy-start = (f32[448,512]{1,0:T(8,128)S(1)}, f32[448,512]{1,0:T(8,128)}, u32[]{:S(2)}) copy-start(f32[448,512]{1,0:T(8,128)} %get-tuple-element.8) | copy-start | bytes 2752516

commit v3 on v2

--- a/solution.py
+++ b/solution.py
@@ -12,7 +12,7 @@
 Z, X, Y, C = 4, 2, 2, 2
 HALVES = 2
 PIECES = 3 * HALVES
-X_FIRST = (0, 3, 4)
+X_FIRST = (0, 3)
 RIGHT, LEFT, ACROSS = 0, 1, 2
 
 
@@ -261,8 +261,12 @@
             else:
                 pl.when(z >= distance - 1)(lambda: project(z - distance + 1, half))
                 pl.when(z + distance - 1 < Z)(lambda: project(z + distance - 1, half))
-            if half == 1:
-                line_round(distance - 1, 0)
+            if half == 1 and distance == 1:
+                keep_terms(0)
+            if half == 1 and distance == 2:
+                line_round(0, 0)
+            if half == 1 and distance == 3:
+                line_round(1, 0)
         pl.when(z == Z - 1)(lambda: project(z - (Z - 1), half))
         pl.when(z == 0)(lambda: project(z + Z - 1, half))
         hidden_gradients(half)
@@ -271,7 +275,8 @@
             for j, to in enumerate(share_targets):
                 share_out[j] = share_term(to)
                 share_copy(j).start()
-        keep_terms(half)
+            line_round(2, 0)
+            keep_terms(1)
 
     share_out[Y * C - 1] = share_term(expert)
     for j in range(Z - 1):

time: 223 us -> 218 us (0.978)
  Pallas kernels: 216 us -> 211 us
    pallas_call x1, Pallas kernels: 216 us -> 211 us  [local_kernel(): pl.pallas_call(functools.partial(kernel, scale), out_shape=(jax.ShapeDtyp...]
where the time goes in v3:
time: 218 us
  Pallas kernels  211 us (97%)
  local copies, waits for them, and re-layouts  5.34 us (2%)
    pallas_call x1, Pallas kernels, local_kernel(): pl.pallas_call(functools.partial(kernel, scale), out_shape=(jax.ShapeDtyp...  211 us
    unnamed x5, local copies, waits for them, and re-layouts  5.34 us

profile of v3, /device:TPU:0, one launch (start us, length us, event | category | flops | bytes accessed | tf_op | source)
XLA Modules:
  0.0 217.7 jit_solution(7643102666622687578)
XLA Ops:
  1.3 211.1 %shard_map.103 = (bf16[512,896]{1,0:T(8,128)(2,1)}, f32[448,512]{1,0:T(8,128)}, f32[448,512]{1,0:T(8,128)}) custom-call(bf16[512,3584]{1,0:T(8,128)(2,1)} %tokens_hbm.1, bf16[512,3584]{1,0:T(8,128)(2,1)} %cotangent_hbm.1, s32[1,512]{1,0:T(1,128)} %bitcast.2, f32[1,512]{1,0:T(1,128)} %bitcast.3, s32[1]{0:T(128)S(6)} %copy.14.count_ref, ...), custom_call_target="tpu_custom_call" | custom-call | flops 13153337344 | bytes 16777216 | tf_op jit(solution)/shard_map/pallas_call | solution.py:353
  212.3 0.0 copy-start
  212.4 2.3 %copy.15 = bf16[512,896]{1,0:T(8,128)(2,1)} copy(bf16[512,896]{1,0:T(8,128)(2,1)} %get-tuple-element.6) | data formatting | bytes 1835008
  214.6 2.2 copy.16
  216.8 0.0 copy-done
  216.8 0.9 copy.17
Async XLA Ops:
  212.3 4.4 %copy-start = (f32[448,512]{1,0:T(8,128)S(1)}, f32[448,512]{1,0:T(8,128)}, u32[]{:S(2)}) copy-start(f32[448,512]{1,0:T(8,128)} %get-tuple-element.8) | copy-start | bytes 2752516
